TPU v7x, 512 devices: a whole 4x8x8 slice. The times are simulated.
512 devices in a mesh: dp: 4 (over y_hi), ctx: 16 (over z, y_lo), exp: 8 (over x, core).
Axes of the slice: x: 4, y: 8 (y_hi: 4, y_lo: 2; y = y_hi * 2 + y_lo), z: 8, core: 2. Of those that a mesh axis runs over, the one named last changes fastest.
Arguments:
- queries: bfloat16 [8192, 4096], P(('dp', 'ctx'), 'exp'), parts along dimension 0, may hold values from -200 to 200
- keys: bfloat16 [8192, 512], P(('dp', 'ctx')), parts along dimension 0, may hold values from -8 to 8
- values: bfloat16 [8192, 512], P(('dp', 'ctx')), parts along dimension 0, may hold values from -6 to 6
- resid: bfloat16 [8192, 2048], P(('dp', 'ctx', 'exp')), parts along dimension 0, may hold values from -3 to 3
- out_proj: bfloat16 [4096, 2048], P('exp'), may hold values from -0.09375 to 0.09375
- norm_gain: float32 [2048], replicated, may hold values from 0.1 to 1.9
- expert_ids: int32 [8192, 8], P(('dp', 'ctx', 'exp')), parts along dimension 0, may hold values from 0 to 15, all different within a row
- gate_probs: float32 [8192, 8], P(('dp', 'ctx', 'exp')), parts along dimension 0, may hold values from 0.02 to 0.4
- w_gate: bfloat16 [16, 2048, 384], P('exp', 'ctx'), may hold values from -0.125 to 0.125
- w_up: bfloat16 [16, 2048, 384], P('exp', 'ctx'), may hold values from -0.125 to 0.125
- w_down: bfloat16 [16, 384, 2048], P('exp', None, 'ctx'), may hold values from -0.3125 to 0.3125
Outputs:
- layer_out: bfloat16 [8192, 2048], P(('dp', 'ctx', 'exp')), parts along dimension 0
There are 4 independent parts, one for each index of `dp`. A program takes and returns all parts, laid end to end along the dimension named above; an argument that names none is the same for every part. Nothing has to cross between parts.
Inputs may be any that keep to these rules, and one draw needn't show every extreme that they name: `expert_ids`: each row names 8 different experts.
All inputs are finite; a program needn't handle non-finite values.
Results may differ from a plain program's by a relative error of at most 0.018.
Values may be sent and summed in bfloat16 or wider, within the bound.
A program may use at most 64 MiB of HBM per device.

v0:
```python
import jax
import jax.numpy as jnp
from jax import lax
from jax.sharding import PartitionSpec as P

QH = 32
KVH = 4
HD = 128
EXPERTS = 16
TOPK = 8


def on_device(
    queries, keys, values, resid, out_proj, norm_gain, expert_ids, gate_probs, w_gate, w_up, w_down
):
    exp_count = lax.axis_size("exp")
    my_index = lax.axis_index("exp")
    local_rows = queries.shape[0]
    local_heads = queries.shape[1] // HD
    head_group = QH // KVH
    kv_count = max(1, local_heads // head_group)
    heads_each = local_heads // kv_count
    scale = float(HD) ** (-0.5)
    first_kv = my_index * local_heads // head_group
    key_cols = lax.dynamic_slice_in_dim(keys, first_kv * HD, kv_count * HD, 1)
    value_cols = lax.dynamic_slice_in_dim(values, first_kv * HD, kv_count * HD, 1)
    packed = jnp.concatenate([key_cols, value_cols], axis=1)
    query_heads = queries.reshape(local_rows, kv_count, heads_each, HD)
    query_first = lax.axis_index("ctx") * local_rows
    query_pos = query_first + jnp.arange(local_rows, dtype=jnp.int32)

    def attend(carry, piece, start):
        piece_rows = piece.shape[0]

        def update(state):
            peak_old, total_old, accum = state
            key_piece = piece[:, : kv_count * HD].reshape(piece_rows, kv_count, HD)
            value_piece = piece[:, kv_count * HD :].reshape(piece_rows, kv_count, HD)
            scores = (
                jnp.einsum(
                    "rghd,kgd->ghrk", query_heads, key_piece, preferred_element_type=jnp.float32
                )
                * scale
            )
            key_pos = start + jnp.arange(piece_rows, dtype=jnp.int32)
            visible = key_pos[None, :] <= query_pos[:, None]
            scores = jnp.where(visible, scores, -1e30)
            peak_new = jnp.maximum(peak_old, jnp.max(scores, axis=3))
            raw = jnp.where(visible, jnp.exp(scores - peak_new[..., None]), 0.0)
            factor = jnp.exp(peak_old - peak_new)
            total_new = total_old * factor + jnp.sum(raw, axis=3)
            mixed = jnp.einsum(
                "ghrk,kgd->ghrd",
                raw.astype(jnp.bfloat16),
                value_piece,
                preferred_element_type=jnp.float32,
            )
            return (peak_new, total_new, accum * factor[..., None] + mixed)

        def unchanged(state):
            return state

        return lax.cond(start <= query_first + local_rows - 1, update, unchanged, carry)

    initial = (
        jnp.full((kv_count, heads_each, local_rows), -1e30, jnp.float32),
        jnp.zeros((kv_count, heads_each, local_rows), jnp.float32),
        jnp.zeros((kv_count, heads_each, local_rows, HD), jnp.float32),
    )
    carry = initial
    piece = lax.all_gather(packed, "ctx", axis=0, tiled=True)
    piece_rows = piece.shape[0]
    blocks = piece.reshape(piece_rows // 512, 512, piece.shape[1])

    def one_block(state, item):
        block_index, block = item
        return (attend(state, block, block_index * 512), None)

    carry, _ = lax.scan(one_block, carry, (jnp.arange(piece_rows // 512, dtype=jnp.int32), blocks))
    _, total_all, accum_all = carry
    attended = (accum_all / total_all[..., None]).astype(jnp.bfloat16)
    attended = jnp.transpose(attended, (2, 0, 1, 3)).reshape(local_rows, local_heads * HD)
    projected = lax.psum_scatter(
        jnp.dot(attended, out_proj, preferred_element_type=jnp.float32).astype(jnp.bfloat16),
        "exp",
        scatter_dimension=0,
        tiled=True,
    ).astype(jnp.float32)
    mid = resid.astype(jnp.float32) + projected
    normed = (
        mid * lax.rsqrt(jnp.mean(mid * mid, axis=1, keepdims=True) + 1e-06) * norm_gain
    ).astype(jnp.bfloat16)
    token_rows = resid.shape[0]
    capacity = (5 * token_rows * TOPK + 4 * EXPERTS - 1) // (4 * EXPERTS)
    flat_ids = expert_ids.reshape(-1)
    onehot = (flat_ids[:, None] == jnp.arange(EXPERTS, dtype=jnp.int32)[None, :]).astype(jnp.int32)
    earlier = jnp.cumsum(onehot, axis=0) - onehot
    rank = jnp.sum(earlier * onehot, axis=1)
    kept = rank < capacity
    target = flat_ids * capacity + rank
    selector = (
        (target[:, None] == jnp.arange(EXPERTS * capacity, dtype=jnp.int32)[None, :])
        & kept[:, None]
    ).astype(jnp.bfloat16)
    token_select = jnp.sum(
        selector.reshape(token_rows, TOPK, EXPERTS * capacity).astype(jnp.float32), axis=1
    ).astype(jnp.bfloat16)
    outgoing = jnp.einsum(
        "ts,td->sd", token_select, normed, preferred_element_type=jnp.float32
    ).astype(jnp.bfloat16)
    arrived = lax.all_to_all(outgoing, "exp", split_axis=0, concat_axis=0, tiled=True)
    experts_here = w_gate.shape[0]
    slot_rows = arrived.reshape(exp_count, experts_here, capacity, arrived.shape[1])
    gate_part = jnp.einsum(
        "sjck,jkf->sjcf",
        slot_rows,
        lax.all_gather(w_gate, "ctx", axis=1, tiled=True),
        preferred_element_type=jnp.float32,
    )
    up_part = jnp.einsum(
        "sjck,jkf->sjcf",
        slot_rows,
        lax.all_gather(w_up, "ctx", axis=1, tiled=True),
        preferred_element_type=jnp.float32,
    )
    hidden = (jax.nn.silu(gate_part) * up_part).astype(jnp.bfloat16)
    produced = jnp.einsum(
        "sjcf,jfk->sjck",
        hidden,
        lax.all_gather(w_down, "ctx", axis=2, tiled=True),
        preferred_element_type=jnp.float32,
    )
    sending_back = produced.astype(jnp.bfloat16).reshape(exp_count * experts_here * capacity, -1)
    returned = lax.all_to_all(sending_back, "exp", split_axis=0, concat_axis=0, tiled=True)
    picked = jnp.dot(selector, returned, preferred_element_type=jnp.float32).reshape(
        token_rows, TOPK, -1
    )
    moe = jnp.sum(picked * gate_probs[:, :, None], axis=1)
    return (mid + moe).astype(jnp.bfloat16)


def solution(mesh):
    placed = (
        P(("dp", "ctx"), "exp"),
        P(("dp", "ctx"), None),
        P(("dp", "ctx"), None),
        P(("dp", "ctx", "exp"), None),
        P("exp", None),
        P(),
        P(("dp", "ctx", "exp"), None),
        P(("dp", "ctx", "exp"), None),
        P("exp", "ctx", None),
        P("exp", "ctx", None),
        P("exp", None, "ctx"),
    )
    return jax.shard_map(
        on_device,
        mesh=mesh,
        in_specs=placed,
        out_specs=P(("dp", "ctx", "exp"), None),
        check_vma=False,
    )
```

profile of v0, /device:TPU:1, one launch (start us, length us, event | category | flops | bytes accessed | tf_op | source)
XLA Modules:
  0.0 436.6 jit_solution(16512700616190216234)
XLA Ops:
  6.5 0.0 copy-start
  6.5 0.0 all-gather.5.cloned.1.call-start
  6.5 0.9 constant_dynamic-slice_fusion
  7.5 0.6 pad_maximum_fusion
  8.1 0.0 all-gather.5.cloned.1.call-update
  8.1 0.0 reduce-scatter.2.cloned.1.call-start
  8.2 1.0 copy.40
  9.2 0.1 copy.41
  9.4 69.4 %all-gather.5.cloned.1.call-done = bf16[2048,256]{1,0:T(8,128)(2,1)} async-done(((bf16[128,256]{1,0:T(8,128)(2,1)}), bf16[2048,256]{1,0:T(8,128)(2,1)}) %all-gather.5.cloned.1.call-update) | async-done | bytes 1048592 | tf_op jit(solution)/shard_map/all_gather | solution.py:71
  78.8 7.3 %while.17 = (s32[]{:T(128)}, f32[1,4,128]{2,1,0:T(4,128)S(1)}, f32[1,4,128]{2,1,0:T(4,128)S(1)}, f32[1,4,128,128]{3,2,1,0:T(8,128)S(1)}, s32[4]{0:T(128)S(1)}, /...) while((s32[]{:T(128)}, f32[1,4,128]{2,1,0:T(4,128)S(1)}, ...), condition=%wide.region_5.6_spmd.clone, body=%wide.region_0.5_spmd.clone.sunk | while | flops 136775808 | bytes 4888863 | solution.py:79
  78.8 0.6 dynamic_slice.26
  80.1 2.2 conditional.3
  80.1 0.1 broadcast_compare_fusion
  80.3 1.0 dynamic-slice_bitcast_fusion
  81.2 0.3 fusion.64
  81.6 0.2 fusion.6
  81.8 0.5 fusion.4
  82.3 0.6 dynamic_slice.26
  83.6 0.6 dynamic_slice.26
  84.9 0.6 dynamic_slice.26
  86.2 0.0 copy-start.3
  86.2 0.0 copy-start.1
  86.2 0.0 copy-start.2
  86.2 0.1 copy.42
  86.4 0.0 copy-done
  86.4 1.3 convolution_convert_fusion.1
  87.6 0.0 reduce-scatter.2.cloned.1.call-update
  87.7 0.0 all-gather.7.cloned.1.call-start
  87.7 0.7 all-gather.7.cloned.1.call-update
  88.4 0.0 all-gather.11.cloned.1.call-start
  88.4 0.5 all-gather.11.cloned.1.call-update
  89.0 0.0 all-gather.9.cloned.1.call-start
  89.0 0.5 all-gather.9.cloned.1.call-update
  89.6 0.0 copy-done.3
  89.6 0.1 copy.43
  89.6 0.1 eq.49
  89.7 0.1 fusion.61
  89.8 0.2 reduce_window_sum.11
  90.0 0.2 select_reduce_fusion
  90.2 0.1 reduce_sum.53
  90.3 0.1 fusion.57
  90.4 45.8 %reduce-scatter.2.cloned.1.call-done = bf16[16,2048]{1,0:T(8,128)(2,1)} async-done(((bf16[128,2048]{1,0:T(8,128)(2,1)}), bf16[16,2048]{1,0:T(8,128)(2,1)}) %reduce-scatter.2.cloned.1.call-update) | async-done | bytes 65552 | tf_op jit(solution)/shard_map/reduce_scatter | solution.py:83
  136.2 0.0 copy-done.1
  136.2 1.0 multiply_reduce_fusion
  137.2 0.0 copy-done.2
  137.2 1.2 convolution_convert_fusion
  138.4 0.1 all_to_all.14
  138.6 17.0 %all_to_all.21 = bf16[8,20,2048]{2,1,0:T(8,128)(2,1)S(1)} all-to-all(bf16[8,20,2048]{2,1,0:T(8,128)(2,1)S(1)} %all_to_all.14), channel_id=1, replica_groups=mesh['dp'=4,'ctx'=16,'exp'=8] {'exp'}, dimensions={0} | all-to-all | bytes 1310720 | tf_op jit(solution)/shard_map/all_to_all | solution.py:111
  155.6 0.4 copy.45
  155.9 63.6 %all-gather.7.cloned.1.call-done = bf16[2,2048,384]{2,1,0:T(8,128)(2,1)} async-done(((bf16[2,128,384]{2,1,0:T(8,128)(2,1)}), bf16[2,2048,384]{2,1,0:T(8,128)(2,1)}) %all-gather.7.cloned.1.call-update) | async-done | bytes 3145744 | tf_op jit(solution)/shard_map/all_gather | solution.py:117
  219.6 2.7 fusion.28
  222.3 87.2 %all-gather.11.cloned.1.call-done = bf16[2,384,2048]{2,1,0:T(8,128)(2,1)} async-done(((bf16[2,384,128]{2,1,0:T(8,128)(2,1)}), bf16[2,384,2048]{2,1,0:T(8,128)(2,1)}) %all-gather.11.cloned.1.call-update) | async-done | bytes 3145744 | tf_op jit(solution)/shard_map/all_gather | solution.py:130
  309.5 87.7 %all-gather.9.cloned.1.call-done = bf16[2,2048,384]{2,1,0:T(8,128)(2,1)} async-done(((bf16[2,128,384]{2,1,0:T(8,128)(2,1)}), bf16[2,2048,384]{2,1,0:T(8,128)(2,1)}) %all-gather.9.cloned.1.call-update) | async-done | bytes 3145744 | tf_op jit(solution)/shard_map/all_gather | solution.py:123
  397.2 5.2 %fusion.24 = bf16[8,2,10,2048]{3,2,0,1:T(8,128)(2,1)} fusion(bf16[2,384,2048]{2,1,0:T(8,128)(2,1)} %all-gather.11.cloned.1.call-done, bf16[2,2048,384]{2,1,0:T(8,128)(2,1)} %all-gather.9.cloned.1.call-done, bf16[8,2,10,2048]{3,0,2,1:T(8,128)(2,1)S(1)} %bitcast.96, f32[8,2,10,384]{3,2,0,1:T(8,128)S(1)} %fusion.28), kind=kOutput, calls=%fused_computation.32 | convolution fusion | flops 504012800 | bytes 7847936 | tf_op jit(solution)/shard_map/sjcf,jfk->sjck/dot_general | solution.py:127
  402.4 0.0 copy-start.4
  402.4 1.6 copy.48
  404.0 1.3 copy.49
  405.3 9.6 %all-to-all-start.1 = ((bf16[8,20,2048]{2,1,0:T(8,128)(2,1)}), bf16[8,20,2048]{2,1,0:T(8,128)(2,1)S(1)}, u32[]{:S(2)}, u32[]{:S(2)}) async-start(bf16[8,20,2048]{2,1,0:T(8,128)(2,1)} %copy.49), calls=%async_computation.2 | async-start | bytes 1572864 | tf_op jit(solution)/shard_map/all_to_all | solution.py:134
  414.9 0.0 copy-done.4
  414.9 0.7 copy.50
  415.6 11.6 %all-to-all-done.1 = bf16[8,20,2048]{2,1,0:T(8,128)(2,1)S(1)} async-done(((bf16[8,20,2048]{2,1,0:T(8,128)(2,1)}), bf16[8,20,2048]{2,1,0:T(8,128)(2,1)S(1)}, u32[]{:S(2)}, u32[]{:S(2)}) %all-to-all-start.1) | async-done | bytes 655392 | tf_op jit(solution)/shard_map/all_to_all | solution.py:134
  427.2 0.1 reshape.141
  427.4 1.2 fusion.27
  428.6 1.5 add_convert_fusion
  (20 shorter events, 0.2 us)
Async XLA Ops:
  6.5 79.8 %copy-start = (bf16[512,2048]{1,0:T(8,128)(2,1)S(1)}, bf16[512,2048]{1,0:T(8,128)(2,1)}, u32[]{:S(2)}) copy-start(bf16[512,2048]{1,0:T(8,128)(2,1)} %param.19) | copy-start | bytes 6291460
  6.5 72.2 %all-gather.5.cloned.1.call-start = ((), (), s32[]{:S(2)}) async-start(), calls=%async_computation.3 | async-start | bytes 1114112 | tf_op jit(solution)/shard_map/all_gather | solution.py:71
  8.1 128.1 %reduce-scatter.2.cloned.1.call-start = ((), (), s32[]{:S(2)}) async-start(), calls=%async_computation.4 | async-start | bytes 589824 | tf_op jit(solution)/shard_map/reduce_scatter | solution.py:83
  86.2 3.4 copy-start.3
  86.2 50.1 %copy-start.1 = (bf16[16,2048]{1,0:T(8,128)(2,1)S(1)}, bf16[16,2048]{1,0:T(8,128)(2,1)}, u32[]{:S(2)}) copy-start(bf16[16,2048]{1,0:T(8,128)(2,1)} %param.18) | copy-start | bytes 196612
  86.2 51.0 %copy-start.2 = (f32[2048]{0:T(1024)S(1)}, f32[2048]{0:T(1024)}, u32[]{:S(2)}) copy-start(f32[2048]{0:T(1024)} %param.20) | copy-start | bytes 24580
  87.7 131.9 %all-gather.7.cloned.1.call-start = ((), (), s32[]{:S(2)}) async-start(), calls=%async_computation.5 | async-start | bytes 3342336 | tf_op jit(solution)/shard_map/all_gather | solution.py:117
  88.4 221.1 %all-gather.11.cloned.1.call-start = ((), (), s32[]{:S(2)}) async-start(), calls=%async_computation.7 | async-start | bytes 3342336 | tf_op jit(solution)/shard_map/all_gather | solution.py:130
  89.0 308.2 %all-gather.9.cloned.1.call-start = ((), (), s32[]{:S(2)}) async-start(), calls=%async_computation.6 | async-start | bytes 3342336 | tf_op jit(solution)/shard_map/all_gather | solution.py:123
  402.4 12.5 %copy-start.4 = (f32[16,8]{0,1:T(8,128)S(1)}, f32[16,8]{0,1:T(8,128)}, u32[]{:S(2)}) copy-start(f32[16,8]{0,1:T(8,128)} %param.22) | copy-start | bytes 1540
  405.3 21.9 %all-to-all-start.1 = ((bf16[8,20,2048]{2,1,0:T(8,128)(2,1)}), bf16[8,20,2048]{2,1,0:T(8,128)(2,1)S(1)}, u32[]{:S(2)}, u32[]{:S(2)}) async-start(bf16[8,20,2048]{2,1,0:T(8,128)(2,1)} %copy.49), calls=%async_computation.2 | async-start | bytes 1572864 | tf_op jit(solution)/shard_map/all_to_all | solution.py:134
Sparse Core Ops, SparseCore 0:
  9.4 69.2 all-gather.4
  87.8 48.4 reduce-scatter.1
  138.5 80.9 all-gather.6
  221.6 87.8 all-gather.10
  311.6 85.5 all-gather.8
where the time goes:
time: 437 us
  waiting for transfers between devices  367 us (84%)
  blocking collectives  17 us (4%)
  between operations  13.3 us (3%)
  matrix products  12.4 us (3%)
  local copies, waits for them, and re-layouts  10 us (2%)
  starting transfers between devices  9.8 us (2%)
    all_gather x1, waiting for transfers between devices, on_device(): lax.all_gather(w_up, 'ctx', axis=1, tiled=True)  87.7 us
    all_gather x1, waiting for transfers between devices, on_device(): lax.all_gather(w_down, 'ctx', axis=2, tiled=True)  87.2 us
    all_gather x1, waiting for transfers between devices, on_device(): piece = lax.all_gather(packed, 'ctx', axis=0, tiled=True)  69.4 us
    all_gather x1, waiting for transfers between devices, on_device(): lax.all_gather(w_gate, 'ctx', axis=1, tiled=True)  63.6 us
    reduce_scatter x1, waiting for transfers between devices, on_device(): lax.psum_scatter(jnp.dot(attended, out_proj, preferred_element_type=jnp.f...  45.8 us
    all_to_all x1, blocking collectives, on_device(): lax.all_to_all(outgoing, 'exp', split_axis=0, concat_axis=0, tiled=True)  17 us
    all_to_all x1, waiting for transfers between devices, on_device(): lax.all_to_all(sending_back, 'exp', split_axis=0, concat_axis=0, tiled=True)  11.6 us
    all_to_all x1, starting transfers between devices, on_device(): lax.all_to_all(sending_back, 'exp', split_axis=0, concat_axis=0, tiled=True)  9.64 us
  transfers between devices with their start and end apart: 6, of which 6 were waited for; matrix products, arithmetic and copies ran while one was open for 2% of the time, Pallas kernels for 0%

commit v1 on v0

v1 whole, which is shorter than its diff:
```python
import functools

import jax
import jax.numpy as jnp
from jax import lax
from jax.experimental import pallas as pl
from jax.experimental.pallas import tpu as pltpu
from jax.sharding import PartitionSpec as P

MESH = pl.DeviceIdType.MESH
BF = jnp.bfloat16
F32 = jnp.float32
HD = 128
D = 2048
FF = 384
NZ = 8
NX = 4
CAP = 10
MSG = D + 128
N_SEM = 160


def layer_kernel(
    q_hbm,
    k_hbm,
    v_hbm,
    resid_hbm,
    op_hbm,
    gain_hbm,
    ids_hbm,
    probs_hbm,
    wg_hbm,
    wu_hbm,
    wd_hbm,
    out_ref,
    q4,
    kv,
    op,
    resid,
    gain,
    ids,
    probs,
    gate_w,
    up_w,
    down_w,
    m_run,
    l_run,
    acc,
    att,
    part,
    part_in,
    part_sum,
    head_in,
    mid_ref,
    rows,
    hid,
    moe,
    moe_in,
    moe_sum,
    moe_x,
    y_out,
    y_in,
    local_sem,
    send_sem,
    recv_sem,
):
    d = lax.axis_index("dp")
    i = lax.axis_index("ctx")
    e = lax.axis_index("exp")
    z, yl = lax.div(i, 2), lax.rem(i, 2)
    x, c = lax.div(e, 2), lax.rem(e, 2)
    role = lax.rem(d, 2)
    y = d * 2 + yl
    y_partner = lax.rem(y + 2 * yl - 1 + 8, 8)

    def zdev(dz):
        return (d, lax.rem(z + dz + NZ, NZ) * 2 + yl, e)

    def xdev(dx):
        return (d, i, lax.rem(x + dx, NX) * 2 + c)

    sibling = (d, i, x * 2 + 1 - c)
    pair = (d, z * 2 + 1 - yl, e)
    partner = (lax.div(y_partner, 2), z * 2 + lax.rem(y_partner, 2), e)

    keys = {}
    sent = []
    locals_ = {}

    def slot(key):
        return keys.setdefault(key, len(keys))

    def send(key, src, dst, device):
        n = slot(key)
        copy = pltpu.make_async_remote_copy(
            src_ref=src,
            dst_ref=dst,
            send_sem=send_sem.at[n],
            recv_sem=recv_sem.at[n],
            device_id=device,
            device_id_type=MESH,
        )
        copy.start()
        sent.append(copy)

    def arrive(key, dst):
        n = slot(key)
        pltpu.make_async_remote_copy(
            src_ref=dst,
            dst_ref=dst,
            send_sem=send_sem.at[n],
            recv_sem=recv_sem.at[n],
            device_id=sibling,
            device_id_type=MESH,
        ).wait_recv()

    def load(key, src, dst):
        copy = pltpu.make_async_copy(src, dst, local_sem.at[len(locals_)])
        copy.start()
        locals_[key] = copy

    def mod_z(dz):
        return lax.rem(z + dz + NZ, NZ)

    own_rows = pl.ds(pl.multiple_of(i * 128, 128), 128)
    head_cols = pl.ds(pl.multiple_of(x * HD, HD), HD)
    load("k", k_hbm.at[:, head_cols], kv.at[0, own_rows])
    load("v", v_hbm.at[:, head_cols], kv.at[1, own_rows])
    for h in range(4):
        load(("q", h), q_hbm.at[:, pl.ds(h * HD, HD)], q4.at[pl.ds(h * HD, HD)])
    load("op", op_hbm, op)
    load("resid", resid_hbm, resid)
    load("gain", gain_hbm, gain)
    load("ids", ids_hbm, ids)
    load("probs", probs_hbm, probs)

    def gate_at(s):
        return gate_w.at[pl.ds(pl.multiple_of(s * 128, 128), 128)]

    def up_at(s):
        return up_w.at[pl.ds(pl.multiple_of(s * 128, 128), 128)]

    def down_at(s):
        return down_w.at[:, pl.ds(pl.multiple_of(s * 128, 128), 128)]

    places = (gate_at, up_at, down_at)
    firsts = (wg_hbm.at[role], wu_hbm.at[role], wd_hbm.at[role])
    for p in range(3):
        load(("w", p), firsts[p], places[p](i))

    barrier = pltpu.get_barrier_semaphore()
    near = [zdev(1), zdev(-1), pair, partner, sibling, xdev(1), xdev(2), xdev(3)]
    for device in near:
        pl.semaphore_signal(barrier, inc=1, device_id=device, device_id_type=MESH)
    pl.semaphore_wait(barrier, len(near))

    def hops(p, w, direction):
        return 4 if ((p + w) % 2 == 0) == (direction > 0) else 3

    def shard(dz, w):
        return mod_z(dz) * 2 + (yl if w == 0 else 1 - yl)

    def weight_z(p, w, direction, hop):
        place = places[p](shard(-direction * hop, w))
        src = firsts[p] if (w == 0 and hop == 0) else place
        send(("wz", p, w, direction, hop), src, place, zdev(direction))

    def weight_y(p, dz):
        place = places[p](shard(dz, 0))
        src = firsts[p] if dz == 0 else place
        send(("wy", p, dz % NZ), src, place, pair)

    def weight_step(p, w, direction, hop):
        place = places[p](shard(-direction * (hop + 1), w))
        arrive(("wz", p, w, direction, hop), place)
        if hop + 1 < hops(p, w, direction):
            weight_z(p, w, direction, hop + 1)
        if p > 0:
            weight_y(p, -direction * (hop + 1))

    events = []
    for hop in range(4):
        for p, w in ((1, 0), (2, 0), (0, 0), (0, 1)):
            for direction in (1, -1):
                if hop < hops(p, w, direction):
                    events.append(functools.partial(weight_step, p, w, direction, hop))

    def pump(n):
        for _ in range(n):
            if events:
                events.pop(0)()

    def kv_at(kind, dz):
        return kv.at[kind, pl.ds(pl.multiple_of(mod_z(dz) * 256, 256), 256)]

    pair_rows = pl.ds(pl.multiple_of((z * 2 + 1 - yl) * 128, 128), 128)

    def kv_hops(direction):
        return 4 if direction > 0 else 3

    def kv_z(direction, hop):
        place = kv_at(c, -direction * hop)
        send(("kz", direction, hop), place, place, zdev(direction))

    locals_["k"].wait()
    locals_["v"].wait()
    send("kp", kv.at[c, own_rows], kv.at[c, own_rows], pair)
    weight_y(0, 0)
    for direction in (1, -1):
        weight_z(1, 0, direction, 0)

    arrive("kp", kv.at[c, pair_rows])
    for direction in (1, -1):
        kv_z(direction, 0)
    send("ks0", kv.at[c, pair_rows], kv.at[c, pair_rows], sibling)
    weight_y(1, 0)
    for direction in (1, -1):
        weight_z(2, 0, direction, 0)

    def block(dz, first):
        key_rows = pl.ds(pl.multiple_of(mod_z(dz) * 256, 256), 256)
        scores = lax.dot_general(
            kv[0, key_rows, :], q4[...], (((1,), (1,)), ((), ())), preferred_element_type=F32
        ) * (float(HD) ** -0.5)
        if first:
            key_pos = z * 256 + lax.broadcasted_iota(jnp.int32, (256, 512), 0)
            query_pos = i * 128 + lax.rem(lax.broadcasted_iota(jnp.int32, (256, 512), 1), 128)
            scores = jnp.where(key_pos <= query_pos, scores, -1e30)
        peak = jnp.max(scores, axis=0, keepdims=True)
        if not first:
            old = m_run[...]
            peak = jnp.maximum(peak, old)
        raw = jnp.exp(scores - peak)
        total = jnp.sum(raw, axis=0, keepdims=True)
        mixed = lax.dot_general(
            kv[1, key_rows, :],
            raw.astype(BF),
            (((0,), (0,)), ((), ())),
            preferred_element_type=F32,
        )
        m_run[...] = peak
        if first:
            l_run[...] = total
            acc[...] = mixed
        else:
            factor = jnp.exp(old - peak)
            l_run[...] = l_run[...] * factor + total
            acc[...] = acc[...] * factor + mixed

    for h in range(4):
        locals_[("q", h)].wait()
    arrive("ks0", kv.at[1 - c, pair_rows])
    block(0, True)

    for hop in range(4):
        around = [s for s in (1, -1) if hop < kv_hops(s)]
        for direction in around:
            place = kv_at(c, -direction * (hop + 1))
            arrive(("kz", direction, hop), place)
            if hop + 1 < kv_hops(direction):
                kv_z(direction, hop + 1)
            send(("ks", direction, hop), place, place, sibling)
        if hop == 0:
            weight_y(2, 0)
            for direction in (1, -1):
                weight_z(0, 0, direction, 0)
        if hop == 1:
            arrive(("wy", 0, 0), gate_at(z * 2 + 1 - yl))
            for direction in (1, -1):
                weight_z(0, 1, direction, 0)
        if hop == 2:
            pump(2)
        for direction in around:
            arrive(("ks", direction, hop), kv_at(1 - c, -direction * (hop + 1)))
        for direction in around:
            dz = -direction * (hop + 1)
            seen = (z + dz >= 0) if direction > 0 else (z + dz >= NZ)
            pl.when(seen)(functools.partial(block, dz, False))

    mixed = acc[...] / l_run[...]
    for h in range(4):
        att[:, h * HD : (h + 1) * HD] = mixed[:, h * HD : (h + 1) * HD].T.astype(BF)
    locals_["op"].wait()

    @pl.loop(0, 4)
    def _(n):
        cols = pl.ds(pl.multiple_of(n * 512, 512), 512)
        share = jnp.dot(att[...], op[:, cols], preferred_element_type=F32).astype(BF)
        for owner in range(8):
            part[owner % 2, owner // 2, :, cols] = share[owner * 16 : owner * 16 + 16]

    send("hs", part.at[1 - c], part_in, sibling)
    pump(2)

    for name in ("ids", "probs", "resid", "gain"):
        locals_[name].wait()
    lane = lax.broadcasted_iota(jnp.int32, (16, 128), 1)
    low = lax.rem(lane, 16)
    chosen = jnp.zeros((16, 128), F32)
    weight = jnp.zeros((16, 128), F32)
    for k in range(8):
        hit = ids[:, k : k + 1] == low
        chosen = jnp.where(hit, 1.0, chosen)
        weight = jnp.where(hit, probs[:, k : k + 1], weight)
    before = (
        lax.broadcasted_iota(jnp.int32, (16, 16), 1) < lax.broadcasted_iota(jnp.int32, (16, 16), 0)
    ).astype(BF)
    rank = jnp.dot(before, chosen.astype(BF), preferred_element_type=F32)
    weight = jnp.where(rank < CAP - 0.5, weight, 0.0)
    high = weight.astype(BF).astype(F32)
    middle = (weight - high).astype(BF).astype(F32)
    least = weight - high - middle
    coded = jnp.where(
        lane < 16, high, jnp.where(lane < 32, middle, jnp.where(lane < 48, least, 0.0))
    )
    rows[0, e, :, D:] = coded.astype(BF)

    arrive("hs", part_in)
    part_sum[...] = (part[c].astype(F32) + part_in[...].astype(F32)).astype(BF)
    for dx in (2, 1, 3):
        send(("hx", dx), part_sum.at[lax.rem(x + dx, NX)], head_in.at[dx - 1], xdev(dx))
    pump(8)
    mid = resid[...].astype(F32) + part_sum[x].astype(F32)
    for dx in (1, 3, 2):
        arrive(("hx", dx), head_in.at[dx - 1])
        mid = mid + head_in[dx - 1].astype(F32)
    mid_ref[...] = mid
    mean = jnp.mean(mid * mid, axis=1, keepdims=True)
    rows[0, e, :, :D] = (mid * lax.rsqrt(mean + 1e-06) * gain[...]).astype(BF)

    own = rows.at[0, e]
    send("ap", own, rows.at[1, e], partner)
    for dx in (2, 1, 3):
        send(("ax", 0, dx), own, own, xdev(dx))
    send(("as", 0, 0), own, own, sibling)
    pump(4)
    other = rows.at[1, e]
    arrive("ap", other)
    for dx in (2, 1, 3):
        send(("ax", 1, dx), other, other, xdev(dx))
    send(("as", 1, 0), other, other, sibling)
    for r in range(2):
        for dx in (1, 3, 2):
            come = rows.at[r, lax.rem(x - dx + NX, NX) * 2 + c]
            arrive(("ax", r, dx), come)
            send(("as", r, dx), come, come, sibling)
        pump(4)
    for r in range(2):
        for dx in range(4):
            arrive(("as", r, dx), rows.at[r, lax.rem(x - dx + NX, NX) * 2 + 1 - c])
    pump(100)
    for p in range(3):
        locals_[("w", p)].wait()

    tokens = rows[:, :, :, :D].reshape(256, D)
    gated = jnp.dot(tokens, gate_w[...], preferred_element_type=F32)
    for dz in range(NZ):
        arrive(("wy", 1, dz), up_at(shard(dz, 1)))
    upped = jnp.dot(tokens, up_w[...], preferred_element_type=F32)
    hid[...] = (gated / (1.0 + jnp.exp(-gated)) * upped).astype(BF)
    codes = rows[:, :, :, D:].reshape(256, 128).astype(F32)
    lanes = lax.broadcasted_iota(jnp.int32, (256, 128), 1)
    mine = (lax.rem(lanes, 16) == e * 2 + role) & (lanes < 48)
    coef = jnp.sum(jnp.where(mine, codes, 0.0), axis=1, keepdims=True)
    for dz in range(NZ):
        arrive(("wy", 2, dz), down_at(shard(dz, 1)))

    @pl.loop(0, 4)
    def _(n):
        cols = pl.ds(pl.multiple_of(n * 512, 512), 512)
        made = jnp.dot(hid[...], down_w[:, cols], preferred_element_type=F32)
        made = (made.astype(BF).astype(F32) * coef).astype(BF)
        for r in range(2):
            for owner in range(8):
                first = r * 128 + owner * 16
                moe[owner % 2, r, owner // 2, :, cols] = made[first : first + 16]

    send("ms", moe.at[1 - c], moe_in, sibling)
    arrive("ms", moe_in)
    for r in (1, 0):
        moe_sum[r] = (moe[c, r].astype(F32) + moe_in[r].astype(F32)).astype(BF)
        for dx in (2, 1, 3):
            send(
                ("mx", r, dx), moe_sum.at[r, lax.rem(x + dx, NX)], moe_x.at[r, dx - 1], xdev(dx)
            )
    total = moe_sum[1, x].astype(F32)
    for dx in (1, 3, 2):
        arrive(("mx", 1, dx), moe_x.at[1, dx - 1])
        total = total + moe_x[1, dx - 1].astype(F32)
    y_out[...] = total.astype(BF)
    send("my", y_out, y_in, partner)
    total = mid_ref[...] + moe_sum[0, x].astype(F32)
    for dx in (1, 3, 2):
        arrive(("mx", 0, dx), moe_x.at[0, dx - 1])
        total = total + moe_x[0, dx - 1].astype(F32)
    for copy in sent:
        copy.wait_send()
    arrive("my", y_in)
    out_ref[...] = (total + y_in[...].astype(F32)).astype(BF)
    assert len(keys) <= N_SEM


def on_device(
    queries, keys, values, resid, out_proj, norm_gain, expert_ids, gate_probs, w_gate, w_up, w_down
):
    anywhere = pl.BlockSpec(memory_space=pl.ANY)
    return pl.pallas_call(
        layer_kernel,
        out_shape=jax.ShapeDtypeStruct((16, D), BF),
        in_specs=[anywhere] * 11,
        out_specs=pl.BlockSpec(memory_space=pltpu.VMEM),
        scratch_shapes=[
            pltpu.VMEM((512, HD), BF),
            pltpu.VMEM((2, 2048, HD), BF),
            pltpu.VMEM((512, D), BF),
            pltpu.VMEM((16, D), BF),
            pltpu.VMEM((1, D), F32),
            pltpu.VMEM((16, 8), jnp.int32),
            pltpu.VMEM((16, 8), F32),
            pltpu.VMEM((D, FF), BF),
            pltpu.VMEM((D, FF), BF),
            pltpu.VMEM((FF, D), BF),
            pltpu.VMEM((1, 512), F32),
            pltpu.VMEM((1, 512), F32),
            pltpu.VMEM((HD, 512), F32),
            pltpu.VMEM((128, 512), BF),
            pltpu.VMEM((2, 4, 16, D), BF),
            pltpu.VMEM((4, 16, D), BF),
            pltpu.VMEM((4, 16, D), BF),
            pltpu.VMEM((3, 16, D), BF),
            pltpu.VMEM((16, D), F32),
            pltpu.VMEM((2, 8, 16, MSG), BF),
            pltpu.VMEM((256, FF), BF),
            pltpu.VMEM((2, 2, 4, 16, D), BF),
            pltpu.VMEM((2, 4, 16, D), BF),
            pltpu.VMEM((2, 4, 16, D), BF),
            pltpu.VMEM((2, 3, 16, D), BF),
            pltpu.VMEM((16, D), BF),
            pltpu.VMEM((16, D), BF),
            pltpu.SemaphoreType.DMA((16,)),
            pltpu.SemaphoreType.DMA((N_SEM,)),
            pltpu.SemaphoreType.DMA((N_SEM,)),
        ],
        compiler_params=pltpu.CompilerParams(
            collective_id=0, has_side_effects=True, vmem_limit_bytes=40 << 20
        ),
        cost_estimate=pl.CostEstimate(
            flops=2_000_000_000, bytes_accessed=6_000_000, transcendentals=1_000_000
        ),
        name="layer",
    )(
        queries,
        keys,
        values,
        resid,
        out_proj,
        norm_gain.reshape(1, D),
        expert_ids,
        gate_probs,
        w_gate,
        w_up,
        w_down,
    )


def solution(mesh):
    placed = (
        P(("dp", "ctx"), "exp"),
        P(("dp", "ctx"), None),
        P(("dp", "ctx"), None),
        P(("dp", "ctx", "exp"), None),
        P("exp", None),
        P(),
        P(("dp", "ctx", "exp"), None),
        P(("dp", "ctx", "exp"), None),
        P("exp", "ctx", None),
        P("exp", "ctx", None),
        P("exp", None, "ctx"),
    )
    return jax.shard_map(
        on_device,
        mesh=mesh,
        in_specs=placed,
        out_specs=P(("dp", "ctx", "exp"), None),
        check_vma=False,
    )
```

time: 437 us -> 86.3 us (0.20)
  waiting for transfers between devices: 367 us -> 0 us
  Pallas kernels: 0 us -> 74.7 us
  blocking collectives: 17 us -> 0 us
  between operations: 13.3 us -> 0.02 us
  matrix products: 12.4 us -> 0 us
  starting transfers between devices: 9.8 us -> 0 us
    all_gather x4 -> x0, waiting for transfers between devices: 308 us -> none  [the longest x1 87.7 us: on_device(): lax.all_gather(w_up, 'ctx', axis=1, tiled=True)]
    pallas_call x0 -> x1, Pallas kernels: none -> 74.7 us  [on_device(): pl.pallas_call(layer_kernel, out_shape=jax.ShapeDtypeStruct((16, D), BF),...]
    reduce_scatter x1 -> x0, waiting for transfers between devices: 45.8 us -> none  [on_device(): lax.psum_scatter(jnp.dot(attended, out_proj, preferred_element_type=jnp.f...]
    all_to_all x1 -> x0, blocking collectives: 17 us -> none  [on_device(): lax.all_to_all(outgoing, 'exp', split_axis=0, concat_axis=0, tiled=True)]
    dot_general x7 -> x0, matrix products: 12.4 us -> none  [the longest x1 5.23 us: on_device(): jnp.einsum('sjcf,jfk->sjck', hidden, lax.all_gather(w_down, 'ctx', axis=2...]
    all_to_all x1 -> x0, waiting for transfers between devices: 11.6 us -> none  [on_device(): lax.all_to_all(sending_back, 'exp', split_axis=0, concat_axis=0, tiled=True)]
    all_to_all x1 -> x0, starting transfers between devices: 9.64 us -> none  [on_device(): lax.all_to_all(sending_back, 'exp', split_axis=0, concat_axis=0, tiled=True)]
    unnamed x14 -> x21, local copies, waits for them, and re-layouts: 1.93 us -> 10.8 us
  transfers between devices with their start and end apart: 6 -> 0, of which waited for: 6 -> 0; matrix products, arithmetic and copies ran while one was open for 2% -> 0% of each run, Pallas kernels for 0% -> 0%
where the time goes in v1:
time: 86.3 us; the launch traced here: 85.5 us
  Pallas kernels  74.7 us (87%)
  local copies, waits for them, and re-layouts  10.8 us (13%)
    pallas_call x1, Pallas kernels, on_device(): pl.pallas_call(layer_kernel, out_shape=jax.ShapeDtypeStruct((16, D), BF),...  74.7 us
    unnamed x21, local copies, waits for them, and re-layouts  10.8 us

profile of v1, /device:TPU:1, one launch (start us, length us, event | category | flops | bytes accessed | tf_op | source)
XLA Modules:
  0.0 85.5 jit_solution(5008351877665734960)
XLA Ops:
  0.0 0.8 copy.12.ids_hbm
  0.8 0.8 copy.13.probs_hbm
  1.5 0.0 copy-start
  1.5 1.6 %copy-done = bf16[512,2048]{1,0:T(8,128)(2,1)S(1)} copy-done((bf16[512,2048]{1,0:T(8,128)(2,1)S(1)}, bf16[512,2048]{1,0:T(8,128)(2,1)}, u32[]{:S(2)}) %copy-start) | copy-done | bytes 2097176
  3.1 0.0 copy-start.1
  3.1 0.9 %copy-done.1 = bf16[2,128,384]{2,1,0:T(8,128)(2,1)S(1)} copy-done((bf16[2,128,384]{2,1,0:T(8,128)(2,1)S(1)}, bf16[2,128,384]{2,1,0:T(8,128)(2,1)}, u32[]{:S(2)}) %copy-start.1) | copy-done | bytes 196632
  4.0 0.0 copy-start.2
  4.0 0.9 %copy-done.2 = bf16[2,128,384]{2,1,0:T(8,128)(2,1)S(1)} copy-done((bf16[2,128,384]{2,1,0:T(8,128)(2,1)S(1)}, bf16[2,128,384]{2,1,0:T(8,128)(2,1)}, u32[]{:S(2)}) %copy-start.2) | copy-done | bytes 196632
  5.0 0.0 copy-start.3
  5.0 0.9 %copy-done.3 = bf16[2,384,128]{2,1,0:T(8,128)(2,1)S(1)} copy-done((bf16[2,384,128]{2,1,0:T(8,128)(2,1)S(1)}, bf16[2,384,128]{2,1,0:T(8,128)(2,1)}, u32[]{:S(2)}) %copy-start.3) | copy-done | bytes 196632
  5.9 0.0 copy-start.4
  5.9 0.9 %copy-done.4 = bf16[128,512]{1,0:T(8,128)(2,1)S(1)} copy-done((bf16[128,512]{1,0:T(8,128)(2,1)S(1)}, bf16[128,512]{1,0:T(8,128)(2,1)}, u32[]{:S(2)}) %copy-start.4) | copy-done | bytes 131096
  6.8 0.0 copy-start.5
  6.8 0.9 %copy-done.5 = bf16[128,512]{1,0:T(8,128)(2,1)S(1)} copy-done((bf16[128,512]{1,0:T(8,128)(2,1)S(1)}, bf16[128,512]{1,0:T(8,128)(2,1)}, u32[]{:S(2)}) %copy-start.5) | copy-done | bytes 131096
  7.7 0.0 copy-start.6
  7.7 0.9 %copy-done.6 = bf16[128,512]{1,0:T(8,128)(2,1)S(1)} copy-done((bf16[128,512]{1,0:T(8,128)(2,1)S(1)}, bf16[128,512]{1,0:T(8,128)(2,1)}, u32[]{:S(2)}) %copy-start.6) | copy-done | bytes 131096
  8.6 0.0 copy-start.7
  8.6 0.8 copy-done.7
  9.4 0.0 copy-start.8
  9.4 0.7 copy-done.8
  10.1 74.7 %layer.1 = bf16[16,2048]{1,0:T(8,128)(2,1)S(1)} custom-call(bf16[128,512]{1,0:T(8,128)(2,1)S(1)} %copy-done.4, bf16[128,512]{1,0:T(8,128)(2,1)S(1)} %copy-done.5, bf16[128,512]{1,0:T(8,128)(2,1)S(1)} %copy-done.6, bf16[16,2048]{1,0:T(8,128)(2,1)S(1)} %copy-done.7, bf16[512,2048]{1,0:T(8,128)(2,1)S(1)} %copy-done, f32[1,2048]{1,0:T(1,128)S(1)} %bitcast.1, ...), custom_call_target="tpu_custom_call" | custom-call | flops 2000000000 | bytes 6000000 | tf_op jit(solution)/shard_map/layer/pallas_call | solution.py:407
  84.9 0.6 copy.15
Async XLA Ops:
  1.5 1.6 %copy-start = (bf16[512,2048]{1,0:T(8,128)(2,1)S(1)}, bf16[512,2048]{1,0:T(8,128)(2,1)}, u32[]{:S(2)}) copy-start(bf16[512,2048]{1,0:T(8,128)(2,1)} %op_hbm.1) | copy-start | bytes 6291460
  3.1 0.9 %copy-start.1 = (bf16[2,128,384]{2,1,0:T(8,128)(2,1)S(1)}, bf16[2,128,384]{2,1,0:T(8,128)(2,1)}, u32[]{:S(2)}) copy-start(bf16[2,128,384]{2,1,0:T(8,128)(2,1)} %wg_hbm.1) | copy-start | bytes 589828
  4.0 0.9 %copy-start.2 = (bf16[2,128,384]{2,1,0:T(8,128)(2,1)S(1)}, bf16[2,128,384]{2,1,0:T(8,128)(2,1)}, u32[]{:S(2)}) copy-start(bf16[2,128,384]{2,1,0:T(8,128)(2,1)} %wu_hbm.1) | copy-start | bytes 589828
  5.0 0.9 %copy-start.3 = (bf16[2,384,128]{2,1,0:T(8,128)(2,1)S(1)}, bf16[2,384,128]{2,1,0:T(8,128)(2,1)}, u32[]{:S(2)}) copy-start(bf16[2,384,128]{2,1,0:T(8,128)(2,1)} %wd_hbm.1) | copy-start | bytes 589828
  5.9 0.9 %copy-start.4 = (bf16[128,512]{1,0:T(8,128)(2,1)S(1)}, bf16[128,512]{1,0:T(8,128)(2,1)}, u32[]{:S(2)}) copy-start(bf16[128,512]{1,0:T(8,128)(2,1)} %q_hbm.1) | copy-start | bytes 393220
  6.8 0.9 %copy-start.5 = (bf16[128,512]{1,0:T(8,128)(2,1)S(1)}, bf16[128,512]{1,0:T(8,128)(2,1)}, u32[]{:S(2)}) copy-start(bf16[128,512]{1,0:T(8,128)(2,1)} %k_hbm.1) | copy-start | bytes 393220
  7.7 0.9 %copy-start.6 = (bf16[128,512]{1,0:T(8,128)(2,1)S(1)}, bf16[128,512]{1,0:T(8,128)(2,1)}, u32[]{:S(2)}) copy-start(bf16[128,512]{1,0:T(8,128)(2,1)} %v_hbm.1) | copy-start | bytes 393220
  8.6 0.8 copy-start.7
  9.4 0.7 copy-start.8

commit v2 on v1

--- a/solution.py
+++ b/solution.py
@@ -18,6 +18,7 @@
 CAP = 10
 MSG = D + 128
 N_SEM = 160
+STEPS = (2, 1, 1, 1, 1, 1, 1, 1, 1, 1, 1, 1, 1, 2, 2, 2, 1)
 
 
 def layer_kernel(
@@ -40,6 +41,7 @@
     gain,
     ids,
     probs,
+    turn,
     gate_w,
     up_w,
     down_w,
@@ -178,15 +180,25 @@
         if p > 0:
             weight_y(p, -direction * (hop + 1))
 
-    events = []
+    def weight_start(p, w):
+        if w == 1:
+            arrive(("wy", p, 0), places[p](shard(0, 1)))
+        for direction in (1, -1):
+            weight_z(p, w, direction, 0)
+
+    def weight_hop(p, w, hop):
+        for direction in (1, -1):
+            if hop < hops(p, w, direction):
+                weight_step(p, w, direction, hop)
+
+    streams = ((1, 0), (2, 0), (0, 0), (0, 1))
+    events = [functools.partial(weight_start, p, w) for p, w in streams]
     for hop in range(4):
-        for p, w in ((1, 0), (2, 0), (0, 0), (0, 1)):
-            for direction in (1, -1):
-                if hop < hops(p, w, direction):
-                    events.append(functools.partial(weight_step, p, w, direction, hop))
-
-    def pump(n):
-        for _ in range(n):
+        events += [functools.partial(weight_hop, p, w, hop) for p, w in streams]
+    points = list(STEPS)
+
+    def point():
+        for _ in range(points.pop(0) if points else len(events)):
             if events:
                 events.pop(0)()
 
@@ -205,17 +217,15 @@
     locals_["k"].wait()
     locals_["v"].wait()
     send("kp", kv.at[c, own_rows], kv.at[c, own_rows], pair)
-    weight_y(0, 0)
-    for direction in (1, -1):
-        weight_z(1, 0, direction, 0)
+    for p in range(3):
+        weight_y(p, 0)
+    point()
 
     arrive("kp", kv.at[c, pair_rows])
     for direction in (1, -1):
         kv_z(direction, 0)
     send("ks0", kv.at[c, pair_rows], kv.at[c, pair_rows], sibling)
-    weight_y(1, 0)
-    for direction in (1, -1):
-        weight_z(2, 0, direction, 0)
+    point()
 
     def block(dz, first):
         key_rows = pl.ds(pl.multiple_of(mod_z(dz) * 256, 256), 256)
@@ -260,22 +270,14 @@
             if hop + 1 < kv_hops(direction):
                 kv_z(direction, hop + 1)
             send(("ks", direction, hop), place, place, sibling)
-        if hop == 0:
-            weight_y(2, 0)
-            for direction in (1, -1):
-                weight_z(0, 0, direction, 0)
-        if hop == 1:
-            arrive(("wy", 0, 0), gate_at(z * 2 + 1 - yl))
-            for direction in (1, -1):
-                weight_z(0, 1, direction, 0)
-        if hop == 2:
-            pump(2)
+        point()
         for direction in around:
             arrive(("ks", direction, hop), kv_at(1 - c, -direction * (hop + 1)))
         for direction in around:
             dz = -direction * (hop + 1)
             seen = (z + dz >= 0) if direction > 0 else (z + dz >= NZ)
             pl.when(seen)(functools.partial(block, dz, False))
+        point()
 
     mixed = acc[...] / l_run[...]
     for h in range(4):
@@ -290,18 +292,23 @@
             part[owner % 2, owner // 2, :, cols] = share[owner * 16 : owner * 16 + 16]
 
     send("hs", part.at[1 - c], part_in, sibling)
-    pump(2)
+    point()
 
     for name in ("ids", "probs", "resid", "gain"):
         locals_[name].wait()
+    turn[...] = jnp.zeros_like(turn)
+    turn[0, :8, :16] = ids[...].astype(F32)
+    turn[1, :8, :16] = probs[...]
+    ids_of = turn[0].T
+    probs_of = turn[1].T
     lane = lax.broadcasted_iota(jnp.int32, (16, 128), 1)
-    low = lax.rem(lane, 16)
+    low = lax.rem(lane, 16).astype(F32)
     chosen = jnp.zeros((16, 128), F32)
     weight = jnp.zeros((16, 128), F32)
     for k in range(8):
-        hit = ids[:, k : k + 1] == low
+        hit = ids_of[:16, k : k + 1] == low
         chosen = jnp.where(hit, 1.0, chosen)
-        weight = jnp.where(hit, probs[:, k : k + 1], weight)
+        weight = jnp.where(hit, probs_of[:16, k : k + 1], weight)
     before = (
         lax.broadcasted_iota(jnp.int32, (16, 16), 1) < lax.broadcasted_iota(jnp.int32, (16, 16), 0)
     ).astype(BF)
@@ -319,9 +326,11 @@
     part_sum[...] = (part[c].astype(F32) + part_in[...].astype(F32)).astype(BF)
     for dx in (2, 1, 3):
         send(("hx", dx), part_sum.at[lax.rem(x + dx, NX)], head_in.at[dx - 1], xdev(dx))
-    pump(8)
+    point()
     mid = resid[...].astype(F32) + part_sum[x].astype(F32)
     for dx in (1, 3, 2):
+        if dx == 2:
+            point()
         arrive(("hx", dx), head_in.at[dx - 1])
         mid = mid + head_in[dx - 1].astype(F32)
     mid_ref[...] = mid
@@ -333,22 +342,23 @@
     for dx in (2, 1, 3):
         send(("ax", 0, dx), own, own, xdev(dx))
     send(("as", 0, 0), own, own, sibling)
-    pump(4)
+    point()
     other = rows.at[1, e]
     arrive("ap", other)
     for dx in (2, 1, 3):
         send(("ax", 1, dx), other, other, xdev(dx))
     send(("as", 1, 0), other, other, sibling)
+    point()
     for r in range(2):
         for dx in (1, 3, 2):
             come = rows.at[r, lax.rem(x - dx + NX, NX) * 2 + c]
             arrive(("ax", r, dx), come)
             send(("as", r, dx), come, come, sibling)
-        pump(4)
+        point()
     for r in range(2):
         for dx in range(4):
             arrive(("as", r, dx), rows.at[r, lax.rem(x - dx + NX, NX) * 2 + 1 - c])
-    pump(100)
+    point()
     for p in range(3):
         locals_[("w", p)].wait()
 
@@ -365,19 +375,20 @@
     for dz in range(NZ):
         arrive(("wy", 2, dz), down_at(shard(dz, 1)))
 
-    @pl.loop(0, 4)
-    def _(n):
-        cols = pl.ds(pl.multiple_of(n * 512, 512), 512)
-        made = jnp.dot(hid[...], down_w[:, cols], preferred_element_type=F32)
-        made = (made.astype(BF).astype(F32) * coef).astype(BF)
-        for r in range(2):
+    for r in (1, 0):
+
+        @pl.loop(0, 4)
+        def _(n):
+            cols = pl.ds(pl.multiple_of(n * 512, 512), 512)
+            own_hid = hid[r * 128 : r * 128 + 128]
+            made = jnp.dot(own_hid, down_w[:, cols], preferred_element_type=F32)
+            made = (made.astype(BF).astype(F32) * coef[r * 128 : r * 128 + 128]).astype(BF)
             for owner in range(8):
-                first = r * 128 + owner * 16
-                moe[owner % 2, r, owner // 2, :, cols] = made[first : first + 16]
-
-    send("ms", moe.at[1 - c], moe_in, sibling)
-    arrive("ms", moe_in)
+                moe[owner % 2, r, owner // 2, :, cols] = made[owner * 16 : owner * 16 + 16]
+
+        send(("ms", r), moe.at[1 - c, r], moe_in.at[r], sibling)
     for r in (1, 0):
+        arrive(("ms", r), moe_in.at[r])
         moe_sum[r] = (moe[c, r].astype(F32) + moe_in[r].astype(F32)).astype(BF)
         for dx in (2, 1, 3):
             send(
@@ -403,11 +414,11 @@
 def on_device(
     queries, keys, values, resid, out_proj, norm_gain, expert_ids, gate_probs, w_gate, w_up, w_down
 ):
-    anywhere = pl.BlockSpec(memory_space=pl.ANY)
+    in_hbm = pl.BlockSpec(memory_space=pltpu.HBM)
     return pl.pallas_call(
         layer_kernel,
         out_shape=jax.ShapeDtypeStruct((16, D), BF),
-        in_specs=[anywhere] * 11,
+        in_specs=[in_hbm] * 11,
         out_specs=pl.BlockSpec(memory_space=pltpu.VMEM),
         scratch_shapes=[
             pltpu.VMEM((512, HD), BF),
@@ -415,8 +426,9 @@
             pltpu.VMEM((512, D), BF),
             pltpu.VMEM((16, D), BF),
             pltpu.VMEM((1, D), F32),
-            pltpu.VMEM((16, 8), jnp.int32),
-            pltpu.VMEM((16, 8), F32),
+            pltpu.VMEM((8, 16), jnp.int32),
+            pltpu.VMEM((8, 16), F32),
+            pltpu.VMEM((2, 128, 128), F32),
             pltpu.VMEM((D, FF), BF),
             pltpu.VMEM((D, FF), BF),
             pltpu.VMEM((FF, D), BF),
@@ -442,7 +454,7 @@
             pltpu.SemaphoreType.DMA((N_SEM,)),
         ],
         compiler_params=pltpu.CompilerParams(
-            collective_id=0, has_side_effects=True, vmem_limit_bytes=40 << 20
+            collective_id=0, has_side_effects=True, vmem_limit_bytes=58 << 20
         ),
         cost_estimate=pl.CostEstimate(
             flops=2_000_000_000, bytes_accessed=6_000_000, transcendentals=1_000_000
@@ -455,8 +467,8 @@
         resid,
         out_proj,
         norm_gain.reshape(1, D),
-        expert_ids,
-        gate_probs,
+        expert_ids.T,
+        gate_probs.T,
         w_gate,
         w_up,
         w_down,

time: 86.3 us -> 72.1 us (0.84)
  local copies, waits for them, and re-layouts: 10.8 us -> 1.47 us
  Pallas kernels: 74.7 us -> 70.5 us
    unnamed x21 -> x1, local copies, waits for them, and re-layouts: 10.8 us -> 1.47 us
    pallas_call x1, Pallas kernels: 74.7 us -> 70.5 us  [on_device(): pl.pallas_call(layer_kernel, out_shape=jax.ShapeDtypeStruct((16, D), BF),...]
where the time goes in v2:
time: 72.1 us; the launch traced here: 71.9 us
  Pallas kernels  70.5 us (98%)
  local copies, waits for them, and re-layouts  1.47 us (2%)
    pallas_call x1, Pallas kernels, on_device(): pl.pallas_call(layer_kernel, out_shape=jax.ShapeDtypeStruct((16, D), BF),...  70.5 us
    unnamed x1, local copies, waits for them, and re-layouts  1.47 us

profile of v2, /device:TPU:1, one launch (start us, length us, event | category | flops | bytes accessed | tf_op | source)
XLA Modules:
  0.0 71.9 jit_solution(10851207092312671385)
XLA Ops:
  0.0 70.5 %layer.1 = bf16[16,2048]{1,0:T(8,128)(2,1)} custom-call(bf16[128,512]{1,0:T(8,128)(2,1)} %q_hbm.1, bf16[128,512]{1,0:T(8,128)(2,1)} %k_hbm.1, bf16[128,512]{1,0:T(8,128)(2,1)} %v_hbm.1, bf16[16,2048]{1,0:T(8,128)(2,1)} %resid_hbm.1, bf16[512,2048]{1,0:T(8,128)(2,1)} %op_hbm.1, f32[1,2048]{1,0:T(1,128)} %bitcast.3, s32[8,16]{1,0:T(8,128)} %bitcast.4, ...), custom_call_target="tpu_custom_call" | custom-call | flops 2000000000 | bytes 6000000 | tf_op jit(solution)/shard_map/layer/pallas_call | solution.py:418
  70.5 1.5 %copy.13 = bf16[16,2048]{1,0:T(8,128)(2,1)} copy(bf16[16,2048]{1,0:T(8,128)(2,1)} %layer.1) | data formatting | bytes 131072

commit v3 on v2

--- a/solution.py
+++ b/solution.py
@@ -18,7 +18,7 @@
 CAP = 10
 MSG = D + 128
 N_SEM = 160
-STEPS = (2, 1, 1, 1, 1, 1, 1, 1, 1, 1, 1, 1, 1, 2, 2, 2, 1)
+STEPS = (2, 1, 1, 1, 1, 1, 1, 1, 1, 1, 1, 2, 0, 2, 2, 2, 1)
 
 
 def layer_kernel(
@@ -56,6 +56,7 @@
     mid_ref,
     rows,
     hid,
+    upped,
     moe,
     moe_in,
     moe_sum,
@@ -87,12 +88,13 @@
 
     keys = {}
     sent = []
+    sent_if = []
     locals_ = {}
 
     def slot(key):
         return keys.setdefault(key, len(keys))
 
-    def send(key, src, dst, device):
+    def send(key, src, dst, device, cond=None):
         n = slot(key)
         copy = pltpu.make_async_remote_copy(
             src_ref=src,
@@ -103,7 +105,10 @@
             device_id_type=MESH,
         )
         copy.start()
-        sent.append(copy)
+        if cond is None:
+            sent.append(copy)
+        else:
+            sent_if.append((cond, n, src.shape[0]))
 
     def arrive(key, dst):
         n = slot(key)
@@ -147,6 +152,7 @@
 
     places = (gate_at, up_at, down_at)
     firsts = (wg_hbm.at[role], wu_hbm.at[role], wd_hbm.at[role])
+    others = (wg_hbm.at[1 - role], wu_hbm.at[1 - role], wd_hbm.at[1 - role])
     for p in range(3):
         load(("w", p), firsts[p], places[p](i))
 
@@ -169,8 +175,10 @@
 
     def weight_y(p, dz):
         place = places[p](shard(dz, 0))
-        src = firsts[p] if dz == 0 else place
-        send(("wy", p, dz % NZ), src, place, pair)
+        if dz == 0:
+            send(("wy", p, 0), others[p], place, partner)
+        else:
+            send(("wy", p, dz % NZ), place, place, pair)
 
     def weight_step(p, w, direction, hop):
         place = places[p](shard(-direction * (hop + 1), w))
@@ -207,12 +215,27 @@
 
     pair_rows = pl.ds(pl.multiple_of((z * 2 + 1 - yl) * 128, 128), 128)
 
-    def kv_hops(direction):
-        return 4 if direction > 0 else 3
+    def kv_got(direction, hop):
+        if direction > 0:
+            return z >= hop + 1
+        return ((z == 7) | (z <= 1), (z >= 6) | (z == 0), z >= 5)[hop]
+
+    def kv_used(direction, hop):
+        return z >= hop + 1 if direction > 0 else z + hop + 1 >= NZ
+
+    def kv_more(direction, hop):
+        if hop == 0:
+            return z <= NZ - 2 if direction > 0 else z <= 2
+        got = kv_got(direction, hop - 1)
+        return got & (z <= NZ - 2) if direction > 0 else got
 
     def kv_z(direction, hop):
-        place = kv_at(c, -direction * hop)
-        send(("kz", direction, hop), place, place, zdev(direction))
+        more = kv_more(direction, hop)
+
+        @pl.when(more)
+        def _():
+            place = kv_at(c, -direction * hop)
+            send(("kz", direction, hop), place, place, zdev(direction), more)
 
     locals_["k"].wait()
     locals_["v"].wait()
@@ -263,20 +286,30 @@
     block(0, True)
 
     for hop in range(4):
-        around = [s for s in (1, -1) if hop < kv_hops(s)]
+        around = (1, -1) if hop < 3 else (1,)
         for direction in around:
-            place = kv_at(c, -direction * (hop + 1))
-            arrive(("kz", direction, hop), place)
-            if hop + 1 < kv_hops(direction):
+            got, used = kv_got(direction, hop), kv_used(direction, hop)
+
+            @pl.when(got)
+            def _():
+                arrive(("kz", direction, hop), kv_at(c, -direction * (hop + 1)))
+
+            if hop + 1 < (4 if direction > 0 else 3):
                 kv_z(direction, hop + 1)
-            send(("ks", direction, hop), place, place, sibling)
+
+            @pl.when(used)
+            def _():
+                place = kv_at(c, -direction * (hop + 1))
+                send(("ks", direction, hop), place, place, sibling, used)
+
         point()
         for direction in around:
-            arrive(("ks", direction, hop), kv_at(1 - c, -direction * (hop + 1)))
-        for direction in around:
-            dz = -direction * (hop + 1)
-            seen = (z + dz >= 0) if direction > 0 else (z + dz >= NZ)
-            pl.when(seen)(functools.partial(block, dz, False))
+
+            @pl.when(kv_used(direction, hop))
+            def _():
+                arrive(("ks", direction, hop), kv_at(1 - c, -direction * (hop + 1)))
+                block(-direction * (hop + 1), False)
+
         point()
 
     mixed = acc[...] / l_run[...]
@@ -358,24 +391,28 @@
     for r in range(2):
         for dx in range(4):
             arrive(("as", r, dx), rows.at[r, lax.rem(x - dx + NX, NX) * 2 + 1 - c])
-    point()
+    while len(events) > 2:
+        events.pop(0)()
     for p in range(3):
         locals_[("w", p)].wait()
-
-    tokens = rows[:, :, :, :D].reshape(256, D)
-    gated = jnp.dot(tokens, gate_w[...], preferred_element_type=F32)
-    for dz in range(NZ):
+    for dz in range(1, NZ):
         arrive(("wy", 1, dz), up_at(shard(dz, 1)))
-    upped = jnp.dot(tokens, up_w[...], preferred_element_type=F32)
-    hid[...] = (gated / (1.0 + jnp.exp(-gated)) * upped).astype(BF)
+    arrive(("wy", 1, 0), up_at(shard(0, 1)))
+    upped[...] = jnp.dot(rows[:, :, :, :D].reshape(256, D), up_w[...], preferred_element_type=F32)
+    while events:
+        events.pop(0)()
     codes = rows[:, :, :, D:].reshape(256, 128).astype(F32)
     lanes = lax.broadcasted_iota(jnp.int32, (256, 128), 1)
     mine = (lax.rem(lanes, 16) == e * 2 + role) & (lanes < 48)
     coef = jnp.sum(jnp.where(mine, codes, 0.0), axis=1, keepdims=True)
-    for dz in range(NZ):
-        arrive(("wy", 2, dz), down_at(shard(dz, 1)))
-
     for r in (1, 0):
+        tokens = rows[r, :, :, :D].reshape(128, D)
+        gated = jnp.dot(tokens, gate_w[...], preferred_element_type=F32)
+        of_row = pl.ds(r * 128, 128)
+        hid[of_row] = (gated / (1.0 + jnp.exp(-gated)) * upped[of_row]).astype(BF)
+        if r == 1:
+            for dz in range(NZ):
+                arrive(("wy", 2, dz), down_at(shard(dz, 1)))
 
         @pl.loop(0, 4)
         def _(n):
@@ -406,6 +443,20 @@
         total = total + moe_x[0, dx - 1].astype(F32)
     for copy in sent:
         copy.wait_send()
+    for cond, n, length in sent_if:
+
+        @pl.when(cond)
+        def _():
+            like = kv.at[0, pl.ds(0, length)]
+            pltpu.make_async_remote_copy(
+                src_ref=like,
+                dst_ref=like,
+                send_sem=send_sem.at[n],
+                recv_sem=recv_sem.at[n],
+                device_id=sibling,
+                device_id_type=MESH,
+            ).wait_send()
+
     arrive("my", y_in)
     out_ref[...] = (total + y_in[...].astype(F32)).astype(BF)
     assert len(keys) <= N_SEM
@@ -443,6 +494,7 @@
             pltpu.VMEM((16, D), F32),
             pltpu.VMEM((2, 8, 16, MSG), BF),
             pltpu.VMEM((256, FF), BF),
+            pltpu.VMEM((256, FF), F32),
             pltpu.VMEM((2, 2, 4, 16, D), BF),
             pltpu.VMEM((2, 4, 16, D), BF),
             pltpu.VMEM((2, 4, 16, D), BF),

time: 72.1 us -> 70 us (0.971); the launches traced: 71.9 us -> 69 us
  Pallas kernels: 70.5 us -> 67.5 us
    pallas_call x1, Pallas kernels: 70.5 us -> 67.5 us  [on_device(): pl.pallas_call(layer_kernel, out_shape=jax.ShapeDtypeStruct((16, D), BF),...]
where the time goes in v3:
time: 70 us; the launch traced here: 69 us
  Pallas kernels  67.5 us (96%)
  local copies, waits for them, and re-layouts  1.47 us (2%)
    pallas_call x1, Pallas kernels, on_device(): pl.pallas_call(layer_kernel, out_shape=jax.ShapeDtypeStruct((16, D), BF),...  67.5 us
    unnamed x1, local copies, waits for them, and re-layouts  1.47 us

profile of v3, /device:TPU:1, one launch (start us, length us, event | category | flops | bytes accessed | tf_op | source)
XLA Modules:
  0.0 69.0 jit_solution(6851067158094298864)
XLA Ops:
  0.0 67.5 %layer.1 = bf16[16,2048]{1,0:T(8,128)(2,1)} custom-call(bf16[128,512]{1,0:T(8,128)(2,1)} %q_hbm.1, bf16[128,512]{1,0:T(8,128)(2,1)} %k_hbm.1, bf16[128,512]{1,0:T(8,128)(2,1)} %v_hbm.1, bf16[16,2048]{1,0:T(8,128)(2,1)} %resid_hbm.1, bf16[512,2048]{1,0:T(8,128)(2,1)} %op_hbm.1, f32[1,2048]{1,0:T(1,128)} %bitcast.3, s32[8,16]{1,0:T(8,128)} %bitcast.4, ...), custom_call_target="tpu_custom_call" | custom-call | flops 2000000000 | bytes 6000000 | tf_op jit(solution)/shard_map/layer/pallas_call | solution.py:469
  67.5 1.5 %copy.13 = bf16[16,2048]{1,0:T(8,128)(2,1)} copy(bf16[16,2048]{1,0:T(8,128)(2,1)} %layer.1) | data formatting | bytes 131072

commit v4 on v3

--- a/solution.py
+++ b/solution.py
@@ -424,6 +424,7 @@
                 moe[owner % 2, r, owner // 2, :, cols] = made[owner * 16 : owner * 16 + 16]
 
         send(("ms", r), moe.at[1 - c, r], moe_in.at[r], sibling)
+    earlier = len(sent)
     for r in (1, 0):
         arrive(("ms", r), moe_in.at[r])
         moe_sum[r] = (moe[c, r].astype(F32) + moe_in[r].astype(F32)).astype(BF)
@@ -431,6 +432,23 @@
             send(
                 ("mx", r, dx), moe_sum.at[r, lax.rem(x + dx, NX)], moe_x.at[r, dx - 1], xdev(dx)
             )
+    for copy in sent[:earlier]:
+        copy.wait_send()
+    del sent[:earlier]
+    for cond, n, length in sent_if:
+
+        @pl.when(cond)
+        def _():
+            like = kv.at[0, pl.ds(0, length)]
+            pltpu.make_async_remote_copy(
+                src_ref=like,
+                dst_ref=like,
+                send_sem=send_sem.at[n],
+                recv_sem=recv_sem.at[n],
+                device_id=sibling,
+                device_id_type=MESH,
+            ).wait_send()
+
     total = moe_sum[1, x].astype(F32)
     for dx in (1, 3, 2):
         arrive(("mx", 1, dx), moe_x.at[1, dx - 1])
@@ -443,20 +461,6 @@
         total = total + moe_x[0, dx - 1].astype(F32)
     for copy in sent:
         copy.wait_send()
-    for cond, n, length in sent_if:
-
-        @pl.when(cond)
-        def _():
-            like = kv.at[0, pl.ds(0, length)]
-            pltpu.make_async_remote_copy(
-                src_ref=like,
-                dst_ref=like,
-                send_sem=send_sem.at[n],
-                recv_sem=recv_sem.at[n],
-                device_id=sibling,
-                device_id_type=MESH,
-            ).wait_send()
-
     arrive("my", y_in)
     out_ref[...] = (total + y_in[...].astype(F32)).astype(BF)
     assert len(keys) <= N_SEM

time: 70 us -> 70 us (level)
  no operation moved by 1% of the time
where the time goes in v4:
time: 70 us; the launch traced here: 69 us
  Pallas kernels  67.5 us (96%)
  local copies, waits for them, and re-layouts  1.47 us (2%)
    pallas_call x1, Pallas kernels, on_device(): pl.pallas_call(layer_kernel, out_shape=jax.ShapeDtypeStruct((16, D), BF),...  67.5 us
    unnamed x1, local copies, waits for them, and re-layouts  1.47 us

profile of v4, /device:TPU:1, one launch (start us, length us, event | category | flops | bytes accessed | tf_op | source)
XLA Modules:
  0.0 69.0 jit_solution(15203933154130881674)
XLA Ops:
  0.0 67.5 %layer.1 = bf16[16,2048]{1,0:T(8,128)(2,1)} custom-call(bf16[128,512]{1,0:T(8,128)(2,1)} %q_hbm.1, bf16[128,512]{1,0:T(8,128)(2,1)} %k_hbm.1, bf16[128,512]{1,0:T(8,128)(2,1)} %v_hbm.1, bf16[16,2048]{1,0:T(8,128)(2,1)} %resid_hbm.1, bf16[512,2048]{1,0:T(8,128)(2,1)} %op_hbm.1, f32[1,2048]{1,0:T(1,128)} %bitcast.3, s32[8,16]{1,0:T(8,128)} %bitcast.4, ...), custom_call_target="tpu_custom_call" | custom-call | flops 2000000000 | bytes 6000000 | tf_op jit(solution)/shard_map/layer/pallas_call | solution.py:473
  67.5 1.5 %copy.13 = bf16[16,2048]{1,0:T(8,128)(2,1)} copy(bf16[16,2048]{1,0:T(8,128)(2,1)} %layer.1) | data formatting | bytes 131072
